TPU v7x, 128 devices: a whole 4x4x4 slice. The times are simulated.
128 devices in a mesh: tm: 32 (over x, z, core), chan: 4 (over y).
Axes of the slice: x: 4, y: 4, z: 4, core: 2. Of those that a mesh axis runs over, the one named last changes fastest.
Arguments:
- record: float32 [32768, 1024], P('tm', 'chan'), may hold values from -120 to 120
- test_matrix: float32 [64, 1024, 128], P(None, 'chan'), may hold values from -0.0234375 to 0.0234375
Outputs:
- basis: float32 [32768, 128], P('tm')
- coeffs: float32 [64, 1024, 128], P('tm', 'chan')
All inputs are finite; a program needn't handle non-finite values.
Results may differ from a plain program's by a relative error of at most 0.00024.
Values sent between devices are 32-bit elements; how exact they have to be, the bound alone decides.
A program may use at most 256 MiB of HBM per device.

v0:
```python
import jax
import jax.numpy as jnp
from jax import lax
from jax.experimental import pallas as pl
from jax.experimental.pallas import tpu as pltpu
from jax.sharding import PartitionSpec as P

F32, BF16 = jnp.float32, jnp.bfloat16
MESH = pl.DeviceIdType.MESH
NX, NZ, NY = 4, 4, 4
LAGS, CH, K = 64, 256, 128
R = 1024
PR = 2 * R
A = 4
KC = 3 * A * CH
KT = 3 * PR + 128
NT_DOT = (((1,), (1,)), ((), ()))
TN_DOT = (((0,), (0,)), ((), ()))
HI = lax.Precision.HIGHEST


def halves(v):
    hi = v.astype(BF16)
    return hi, (v - hi.astype(F32)).astype(BF16)


def body(rec, w, basis_o, coef_o, xe, wf, xcat, rhs, yb, acc, ry, s_ext, xt, srhs, cp,
         xr, p1, pz, qz, q1, raw, gm, gx, gz, gb, gw, li, lsem, ss, rs):
    tm = lax.axis_index("tm")
    y = lax.axis_index("chan")
    h = tm % 2
    chip = tm // 2
    z = chip % NZ
    x = chip // NZ

    def at(xx, zz, hh):
        return (xx * NZ + zz) * 2 + hh

    sib = at(x, z, 1 - h)
    xn = [at((x + d) % NX, z, h) for d in range(NX)]
    zn = [at(x, (z + d) % NZ, h) for d in range(NZ)]
    yn = [(y + d) % NY for d in range(NY)]

    def send(src, dst, k, dt, dy):
        return pltpu.make_async_remote_copy(src_ref=src, dst_ref=dst, send_sem=ss.at[k], recv_sem=rs.at[k],
                                            device_id=(dt, dy), device_id_type=MESH)

    def arrived(ref, k):
        send(ref, ref, k, sib, y).wait_recv()

    count = [0]

    def sem():
        count[0] += 1
        return count[0] - 1

    own0 = pl.multiple_of(R * h, R)
    lx = pltpu.make_async_copy(rec, xe.at[pl.ds(own0, R)], lsem.at[0])
    lx.start()
    wcopies = []
    for p in range(8):
        for a in range(A):
            c = pltpu.make_async_copy(w.at[pl.ds(16 * a + 2 * p, 2)], wf.at[p, a], lsem.at[1 + 4 * p + a])
            c.start()
            wcopies.append(c)

    bar = pltpu.get_barrier_semaphore()

    def greet(dt, dy):
        pl.semaphore_signal(bar, inc=1, device_id=(dt, dy), device_id_type=MESH)

    greet(sib, y)
    for d in range(1, 4):
        greet(tm, yn[d])
        greet(sib, yn[d])
        greet(xn[d], y)
        greet(zn[d], y)
    gives = jnp.logical_and(h == 0, chip > 0)
    takes = chip < NX * NZ - 1
    down0, down1 = lax.max(tm - 2, 0), lax.max(tm - 1, 0)
    up = lax.min(2 * chip + 2, 2 * NX * NZ - 2)

    @pl.when(gives)
    def _():
        greet(down0, y)
        greet(down1, y)

    @pl.when(takes)
    def _():
        greet(up, y)

    pl.semaphore_wait(bar, 13 + jnp.where(gives, 2, 0) + jnp.where(takes, 1, 0))

    kh0, kh1, ks0, ks1 = sem(), sem(), sem(), sem()
    halo = xe.at[pl.ds(PR, 64)]
    heads = [send(rec.at[pl.ds(0, 64)], xe.at[pl.ds(own0, 64)], ks0, sib, y),
             send(rec.at[pl.ds(64, R - 64)], xe.at[pl.ds(pl.multiple_of(own0 + 64, 64), R - 64)], ks1, sib, y)]
    halos = [pltpu.make_async_remote_copy(src_ref=rec.at[pl.ds(0, 64)], dst_ref=halo, send_sem=ss.at[kk],
                                          recv_sem=rs.at[kh0], device_id=(dd, y), device_id_type=MESH)
             for kk, dd in ((kh0, down0), (kh1, down1))]
    heads[0].start()

    @pl.when(gives)
    def _():
        halos[0].start()
        halos[1].start()

    heads[1].start()

    def prep_w(p, slot):
        for a in range(A):
            for j in range(2):
                hi, lo = halves(wf[p, a, j])
                cs = pl.ds(128 * j, 128)
                rhs[slot, pl.ds(a * CH, CH), cs] = hi
                rhs[slot, pl.ds((A + a) * CH, CH), cs] = lo
                rhs[slot, pl.ds((2 * A + a) * CH, CH), cs] = hi

    for c in wcopies[:4]:
        c.wait()
    prep_w(0, 0)
    acc[...] = jnp.zeros_like(acc)
    zpad = jnp.zeros((16, K), F32)
    s_ext[pl.ds(0, 16)] = zpad
    s_ext[pl.ds(16 + PR, 16)] = zpad
    lx.wait()
    oth0 = pl.multiple_of(R - R * h, R)

    @pl.when(jnp.logical_not(takes))
    def _():
        halo[...] = jnp.zeros((64, CH), F32)

    @pl.when(takes)
    def _():
        arrived(halo, kh0)

    arrived(xe.at[pl.ds(oth0, 64)], ks0)

    @pl.loop(0, 13)
    def _(i):
        for a in range(A):
            hi, lo = halves(xe[pl.ds(pl.multiple_of(R * h + 80 * i + 16 * a, 16), 80), :])
            rows = pl.ds(pl.multiple_of(80 * i, 16), 80)
            xcat[rows, pl.ds(a * CH, CH)] = hi
            xcat[rows, pl.ds((A + a) * CH, CH)] = hi
            xcat[rows, pl.ds((2 * A + a) * CH, CH)] = lo

    for c in wcopies[4:]:
        c.wait()

    @pl.loop(0, 8)
    def _(p):
        slot = p % 2
        res = jnp.dot(xcat[...], rhs[slot], preferred_element_type=F32)
        yb[0] = res[:, :K]
        yb[1] = res[:, K:]
        prep_w(lax.min(p + 1, 7), 1 - slot)
        acc[...] += yb[0, pl.ds(2 * p, R), :] + yb[1, pl.ds(2 * p + 1, R), :]

    kry = [sem() for _ in range(3)]
    outs = []
    for d in (2, 1, 3):
        c = send(acc.at[pl.ds(pl.multiple_of(yn[d] * 256, 256), 256)], ry.at[d - 1], kry[d - 1], tm, yn[d])
        c.start()
        outs.append(c)
    arrived(xe.at[pl.ds(pl.multiple_of(oth0 + 64, 64), R - 64)], ks1)

    def xprep(i):
        cols = pl.multiple_of(128 * i, 128)
        for a in range(A):
            v = xe[pl.ds(pl.multiple_of(128 * i + 16 * a, 16), 128), :].T
            hi, lo = halves(v)
            rows = pl.ds(a * CH, CH)
            xt[rows, pl.ds(cols, 128)] = hi
            xt[rows, pl.ds(pl.multiple_of(PR + cols, 128), 128)] = hi
            xt[rows, pl.ds(pl.multiple_of(2 * PR + cols, 128), 128)] = lo

    for a in range(A):
        v = xe[pl.ds(PR + 16 * a, 16), :]
        hi = v.astype(BF16).astype(F32)
        t = jnp.concatenate([hi, hi, v - hi, jnp.zeros((80, CH), F32)], axis=0)
        xt[pl.ds(a * CH, CH), pl.ds(3 * PR, 128)] = t.T.astype(BF16)
    pl.loop(0, 8)(xprep)
    for d in range(1, 4):
        arrived(ry.at[d - 1], kry[d - 1])
    own_q = pl.ds(pl.multiple_of(y * 256, 256), 256)
    mine = pl.ds(pl.multiple_of(16 + R * h + 256 * y, 16), 256)
    s_ext[mine] = (acc[own_q] + ry[0]) + (ry[1] + ry[2])

    kag = [sem() for _ in range(3)]
    kfw = [sem() for _ in range(4)]

    def place(hh, yy):
        return s_ext.at[pl.ds(pl.multiple_of(16 + R * hh + 256 * yy, 16), 256)]

    for d in (2, 1, 3):
        c = send(place(h, y), place(h, y), kag[d - 1], tm, yn[d])
        c.start()
        outs.append(c)
    c = send(place(h, y), place(h, y), kfw[0], sib, y)
    c.start()
    outs.append(c)
    pl.loop(8, 16)(xprep)
    for d in (1, 3, 2):
        src = place(h, (y + 4 - d) % NY)
        arrived(src, kag[d - 1])
        c = send(src, src, kfw[d], sib, y)
        c.start()
        outs.append(c)
    for d in range(4):
        arrived(place(1 - h, (y + 4 - d) % NY), kfw[d])

    def prep_s(b0, slot):
        for j in range(2):
            cs = pl.ds(128 * j, 128)

            @pl.loop(0, 16)
            def _(i):
                hi, lo = halves(s_ext[pl.ds(128 * i + 16 - b0 - j, 128), :])
                o = pl.multiple_of(128 * i, 128)
                srhs[slot, pl.ds(o, 128), cs] = hi
                srhs[slot, pl.ds(pl.multiple_of(PR + o, 128), 128), cs] = lo
                srhs[slot, pl.ds(pl.multiple_of(2 * PR + o, 128), 128), cs] = hi

            v = s_ext[pl.ds(PR + 16 - b0 - j, 16), :]
            hi, lo = halves(v)
            srhs[slot, pl.ds(3 * PR, 16), cs] = hi
            srhs[slot, pl.ds(3 * PR + 16, 16), cs] = lo
            srhs[slot, pl.ds(3 * PR + 32, 16), cs] = hi
            srhs[slot, pl.ds(3 * PR + 48, 80), cs] = jnp.zeros((80, K), BF16)

    order = (2, 1, 3, 0)

    def tile(t, zd):
        prep_s(4 * zd + 2 * h, 0)
        for half in range(2):
            rows = pl.ds(512 * half, 512)
            res = jnp.dot(xt[rows, :], srhs[0], preferred_element_type=F32)
            cp[t, 0, rows, :] = res[:, :K]
            cp[t, 1, rows, :] = res[:, K:]

    def blk(i, ab=None):
        if ab is None:
            return pl.ds(pl.multiple_of(i * CH, CH), CH)
        return pl.ds(pl.multiple_of(i * CH + 128 * ab, 128), 128)

    xk = [[sem() for _ in range(6)] for _ in range(5)]
    xp, xm, xo = (x + 1) % 4, (x + 3) % 4, (x + 2) % 4

    def go(src, dst, k, dt):
        c = send(src, dst, k, dt, y)
        c.start()
        outs.append(c)

    def x_first(n, src):
        go(src.at[blk(xo, 0)], xr.at[n, 0], xk[n][0], xn[1])
        go(src.at[blk(xo, 1)], xr.at[n, 1], xk[n][1], xn[3])
        go(src.at[blk(xm, 0)], xr.at[n, 2], xk[n][2], xn[3])
        go(src.at[blk(xp, 1)], xr.at[n, 3], xk[n][3], xn[1])

    def x_second(n, src):
        arrived(xr.at[n, 0], xk[n][0])
        src[blk(xp, 0)] += xr[n, 0]
        go(src.at[blk(xp, 0)], xr.at[n, 4], xk[n][4], xn[1])
        arrived(xr.at[n, 1], xk[n][1])
        src[blk(xm, 1)] += xr[n, 1]
        go(src.at[blk(xm, 1)], xr.at[n, 5], xk[n][5], xn[3])

    def x_last(n, src, dst):
        arrived(xr.at[n, 2], xk[n][2])
        arrived(xr.at[n, 3], xk[n][3])
        arrived(xr.at[n, 4], xk[n][4])
        arrived(xr.at[n, 5], xk[n][5])
        dst[0:128] = src[blk(x, 0)] + (xr[n, 2] + xr[n, 4])
        dst[128:256] = src[blk(x, 1)] + (xr[n, 3] + xr[n, 5])

    zk = [[sem() for _ in range(6)] for _ in range(2)]

    def z_part(t, src, buf, ks, dst=None):
        half = buf.shape[1]
        a, b = pl.ds(0, half), pl.ds(half, half)
        if t == 0:
            go(src.at[a], buf.at[0], ks[0], zn[1])
            go(src.at[b], buf.at[1], ks[1], zn[3])
        elif t == 1:
            go(src.at[b], buf.at[3], ks[3], zn[1])
            arrived(buf.at[0], ks[0])
            src[a] += buf[0]
            go(src.at[a], buf.at[4], ks[4], zn[1])
        elif t == 2:
            go(src.at[a], buf.at[2], ks[2], zn[3])
            arrived(buf.at[1], ks[1])
            src[b] += buf[1]
            go(src.at[b], buf.at[5], ks[5], zn[3])
        else:
            for i in (2, 3, 4, 5):
                arrived(buf.at[i], ks[i])
            dst[a] = src[a] + (buf[2] + buf[4])
            dst[b] = src[b] + (buf[3] + buf[5])

    kgx = [sem() for _ in range(3)]
    kgz = [sem() for _ in range(3)]
    kgb = [sem() for _ in range(7)]
    piece = pl.ds(pl.multiple_of((h * NY + y) * 16, 16), 16)

    def zdest(t):
        return (z + order[t]) % NZ

    def pt(t):
        return cp.at[t, 0]

    def qt(t):
        return cp.at[t, 1]

    tile(0, zdest(0))
    x_first(0, pt(0))
    z_part(0, qt(0), qz, zk[1])
    sv = s_ext[pl.ds(16, PR), :]
    gm[...] = lax.dot_general(sv, sv, TN_DOT, precision=HI, preferred_element_type=F32)
    for d in range(1, 4):
        go(gm.at[piece], gx.at[d - 1], kgx[d - 1], xn[d])
    tile(1, zdest(1))
    z_part(1, qt(1), qz, zk[1])
    x_first(1, pt(1))
    x_second(0, pt(0))
    for d in range(1, 4):
        arrived(gx.at[d - 1], kgx[d - 1])
    gz[3] = sum_in_order(gm[piece], gx, x)
    for d in range(1, 4):
        go(gz.at[3], gz.at[d - 1], kgz[d - 1], zn[d])
    tile(2, zdest(2))
    z_part(2, qt(2), qz, zk[1])
    x_first(2, pt(2))
    x_second(1, pt(1))
    x_last(0, pt(0), p1.at[0])
    z_part(0, p1.at[0], pz, zk[0])
    for d in range(1, 4):
        arrived(gz.at[d - 1], kgz[d - 1])
    gb[piece] = sum_in_order(gz[3], gz, z)
    for i, (dt, dy) in enumerate([(tm, yn[1]), (tm, yn[2]), (tm, yn[3]), (sib, y), (sib, yn[1]), (sib, yn[2]), (sib, yn[3])]):
        c = send(gb.at[piece], gb.at[piece], kgb[i], dt, dy)
        c.start()
        outs.append(c)
    tile(3, zdest(3))
    x_first(3, pt(3))
    x_second(2, pt(2))
    z_part(3, qt(3), qz, zk[1], q1)
    x_first(4, q1)
    x_last(1, pt(1), p1.at[1])
    z_part(1, p1.at[1], pz, zk[0])
    x_second(3, pt(3))
    for i in range(7):
        d = (0, 1, 2, 3)[(i + 1) % 4] if i < 3 else i - 3
        hh = h if i < 3 else 1 - h
        arrived(gb.at[pl.ds(pl.multiple_of((hh * NY + (y + 4 - d) % NY) * 16, 16), 16)], kgb[i])
    gw[...] = gb[...]
    factor(gw, li)
    x_last(2, pt(2), p1.at[2])
    z_part(2, p1.at[2], pz, zk[0])
    x_second(4, q1)
    root = float(NX * NZ * PR) ** 0.5
    own_s = s_ext[pl.ds(pl.multiple_of(16 + R * h, 16), R), :]
    basis_o[...] = lax.dot_general(own_s, li[...], NT_DOT, precision=HI, preferred_element_type=F32) * root
    x_last(3, pt(3), p1.at[3])
    z_part(3, p1.at[3], pz, zk[0], raw.at[0])
    x_last(4, q1, raw.at[1])
    for j in range(2):
        coef_o[j] = lax.dot_general(raw[j], li[...], NT_DOT, precision=HI, preferred_element_type=F32)

    for c in outs:
        c.wait_send()
    heads[0].wait_send()
    heads[1].wait_send()

    @pl.when(gives)
    def _():
        halos[0].wait_send()
        halos[1].wait_send()


def sum_in_order(own, bufs, me):
    total = None
    for pos in range(4):
        v = jnp.where(me == pos, own, jnp.zeros_like(own))
        for d in range(1, 4):
            v = v + jnp.where((me + 4 - d) % 4 == pos, bufs[d - 1], jnp.zeros_like(own))
        total = v if total is None else total + v
    return total


def factor(g, li):
    rows = lax.broadcasted_iota(jnp.int32, (K, K), 0)
    cols = lax.broadcasted_iota(jnp.int32, (K, K), 1)
    li[...] = jnp.where(rows == cols, 1.0, 0.0).astype(F32)

    @pl.loop(0, K // 8)
    def _(jb):
        base = pl.multiple_of(jb * 8, 8)
        for j in range(8):
            pa = g[pl.ds(base, 8), :][j : j + 1, :]
            pb = li[pl.ds(base, 8), :][j : j + 1, :]
            r = lax.rsqrt(pa[:, j : j + 1])
            ra = pa * r
            rb = pb * r
            av = g[...]
            f = jnp.where(rows[:, :1] > base + j, av[:, j : j + 1] * r, 0.0)
            g[...] = av - f * ra
            li[...] = jnp.where(rows == base + j, rb, li[...] - f * rb)
        g[...] = pltpu.roll(g[...], K - 8, 1)


N_SEM = 4 + 3 + 3 + 4 + 30 + 12 + 3 + 3 + 7


def on_device(record, test_matrix):
    V = pl.BlockSpec(memory_space=pltpu.VMEM)
    H = pl.BlockSpec(memory_space=pl.ANY)
    return pl.pallas_call(
        body,
        out_shape=(jax.ShapeDtypeStruct((R, K), F32), jax.ShapeDtypeStruct((2, CH, K), F32)),
        in_specs=[H, H],
        out_specs=(V, V),
        scratch_shapes=[
            pltpu.VMEM((PR + 64, CH), F32),
            pltpu.VMEM((8, A, 2, CH, K), F32),
            pltpu.VMEM((R + 16, KC), BF16),
            pltpu.VMEM((2, KC, 2 * K), BF16),
            pltpu.VMEM((2, R + 16, K), F32),
            pltpu.VMEM((R, K), F32),
            pltpu.VMEM((3, 256, K), F32),
            pltpu.VMEM((PR + 32, K), F32),
            pltpu.VMEM((A * CH, KT), BF16),
            pltpu.VMEM((1, KT, 2 * K), BF16),
            pltpu.VMEM((4, 2, A * CH, K), F32),
            pltpu.VMEM((5, 6, 128, K), F32),
            pltpu.VMEM((4, CH, K), F32),
            pltpu.VMEM((6, 128, K), F32),
            pltpu.VMEM((6, 512, K), F32),
            pltpu.VMEM((A * CH, K), F32),
            pltpu.VMEM((2, CH, K), F32),
            pltpu.VMEM((K, K), F32),
            pltpu.VMEM((3, 16, K), F32),
            pltpu.VMEM((4, 16, K), F32),
            pltpu.VMEM((K, K), F32),
            pltpu.VMEM((K, K), F32),
            pltpu.VMEM((K, K), F32),
            pltpu.SemaphoreType.DMA((33,)),
            pltpu.SemaphoreType.DMA((N_SEM,)),
            pltpu.SemaphoreType.DMA((N_SEM,)),
        ],
        compiler_params=pltpu.CompilerParams(collective_id=0, has_side_effects=True, vmem_limit_bytes=60 * 2**20),
    )(record, test_matrix)


def solution(mesh):
    return jax.shard_map(
        on_device,
        mesh=mesh,
        in_specs=(P("tm", "chan"), P(None, "chan", None)),
        out_specs=(P("tm", None), P("tm", "chan", None)),
        check_vma=False,
    )
```

profile of v0, /device:TPU:0, one launch (start us, length us, event | category | flops | bytes accessed | tf_op | source)
XLA Modules:
  0.0 103.1 jit_solution(2097979253924375692)
XLA Ops:
  0.6 98.9 %shard_map.41 = (f32[1024,128]{1,0:T(8,128)}, f32[2,256,128]{2,1,0:T(8,128)}) custom-call(f32[1024,256]{1,0:T(8,128)} %rec.1, f32[64,256,128]{2,1,0:T(8,128)} %w.1), custom_call_target="tpu_custom_call" | custom-call | tf_op jit(solution)/shard_map/pallas_call | solution.py:418
  99.6 1.9 %copy.6 = f32[1024,128]{1,0:T(8,128)} copy(f32[1024,128]{1,0:T(8,128)} %get-tuple-element.4) | data formatting | bytes 1048576
  101.4 1.7 %copy.7 = f32[2,256,128]{2,1,0:T(8,128)} copy(f32[2,256,128]{2,1,0:T(8,128)} %get-tuple-element.5) | data formatting | bytes 524288
where the time goes:
time: 103 us
  Pallas kernels  98.9 us (96%)
  local copies, waits for them, and re-layouts  3.54 us (3%)
    pallas_call x1, Pallas kernels, on_device(): pl.pallas_call(body, out_shape=(jax.ShapeDtypeStruct((R, K), F32), jax.Sh...  98.9 us
    unnamed x2, local copies, waits for them, and re-layouts  3.54 us

commit v1 on v0

v1 whole, which is shorter than its diff:
```python
import jax
import jax.numpy as jnp
from jax import lax
from jax.experimental import pallas as pl
from jax.experimental.pallas import tpu as pltpu
from jax.sharding import PartitionSpec as P

F32, BF16 = jnp.float32, jnp.bfloat16
MESH = pl.DeviceIdType.MESH
NX, NZ, NY = 4, 4, 4
LAGS, CH, K = 64, 256, 128
R = 1024
PR = 2 * R
A = 4
KC = 3 * A * CH
KT = 3 * PR + 128
NT_DOT = (((1,), (1,)), ((), ()))
TN_DOT = (((0,), (0,)), ((), ()))
HI = lax.Precision.HIGHEST


def halves(v):
    hi = v.astype(BF16)
    return hi, (v - hi.astype(F32)).astype(BF16)


def body(rec, w, basis_o, coef_o, xe, wf, xcat, rhs, yb, acc, ry, s_ext, xt, srhs, cp,
         xr, p1, q1, pz, qz, raw, gm, ge, gx, gz, gb, gw, li, lsem, ss, rs):
    tm = lax.axis_index("tm")
    y = lax.axis_index("chan")
    h = tm % 2
    chip = tm // 2
    z = chip % NZ
    x = chip // NZ

    def at(xx, zz, hh):
        return (xx * NZ + zz) * 2 + hh

    sib = at(x, z, 1 - h)
    xn = [at((x + d) % NX, z, h) for d in range(NX)]
    zn = [at(x, (z + d) % NZ, h) for d in range(NZ)]
    yn = [(y + d) % NY for d in range(NY)]

    def send(src, dst, k, dt, dy):
        return pltpu.make_async_remote_copy(src_ref=src, dst_ref=dst, send_sem=ss.at[k], recv_sem=rs.at[k],
                                            device_id=(dt, dy), device_id_type=MESH)

    def arrived(ref, k):
        send(ref, ref, k, sib, y).wait_recv()

    count = [0]

    def sem():
        count[0] += 1
        return count[0] - 1

    own0 = pl.multiple_of(R * h, R)
    lx = pltpu.make_async_copy(rec, xe.at[pl.ds(own0, R)], lsem.at[0])
    lx.start()
    wcopies = []
    for p in range(8):
        for a in range(A):
            c = pltpu.make_async_copy(w.at[pl.ds(16 * a + 2 * p, 2)], wf.at[p, a], lsem.at[1 + 4 * p + a])
            c.start()
            wcopies.append(c)

    bar = pltpu.get_barrier_semaphore()

    def greet(dt, dy):
        pl.semaphore_signal(bar, inc=1, device_id=(dt, dy), device_id_type=MESH)

    greet(sib, y)
    for d in range(1, 4):
        greet(tm, yn[d])
        greet(sib, yn[d])
        greet(xn[d], y)
        greet(zn[d], y)
    gives = jnp.logical_and(h == 0, chip > 0)
    takes = chip < NX * NZ - 1
    down0, down1 = lax.max(tm - 2, 0), lax.max(tm - 1, 0)
    up = lax.min(2 * chip + 2, 2 * NX * NZ - 2)

    @pl.when(gives)
    def _():
        greet(down0, y)
        greet(down1, y)

    @pl.when(takes)
    def _():
        greet(up, y)

    def prep_w(p, slot):
        for a in range(A):
            for j in range(2):
                hi, lo = halves(wf[p, a, j])
                cs = pl.ds(128 * j, 128)
                rhs[slot, pl.ds(a * CH, CH), cs] = hi
                rhs[slot, pl.ds((A + a) * CH, CH), cs] = lo
                rhs[slot, pl.ds((2 * A + a) * CH, CH), cs] = hi

    def prep_x(i):
        for a in range(A):
            hi, lo = halves(xe[pl.ds(pl.multiple_of(R * h + 80 * i + 16 * a, 16), 80), :])
            rows = pl.ds(pl.multiple_of(80 * i, 16), 80)
            xcat[rows, pl.ds(a * CH, CH)] = hi
            xcat[rows, pl.ds((A + a) * CH, CH)] = hi
            xcat[rows, pl.ds((2 * A + a) * CH, CH)] = lo

    acc[...] = jnp.zeros_like(acc)
    zpad = jnp.zeros((16, K), F32)
    s_ext[pl.ds(0, 16)] = zpad
    s_ext[pl.ds(16 + PR, 16)] = zpad
    lx.wait()
    pl.loop(0, 12)(prep_x)
    for c in wcopies[:4]:
        c.wait()
    prep_w(0, 0)
    pl.semaphore_wait(bar, 13 + jnp.where(gives, 2, 0) + jnp.where(takes, 1, 0))

    kh0, kh1, ks0, ks1 = sem(), sem(), sem(), sem()
    halo = xe.at[pl.ds(PR, 64)]
    heads = [send(rec.at[pl.ds(0, 64)], xe.at[pl.ds(own0, 64)], ks0, sib, y),
             send(rec.at[pl.ds(64, R - 64)], xe.at[pl.ds(pl.multiple_of(own0 + 64, 64), R - 64)], ks1, sib, y)]
    halos = [pltpu.make_async_remote_copy(src_ref=rec.at[pl.ds(0, 64)], dst_ref=halo, send_sem=ss.at[kk],
                                          recv_sem=rs.at[kh0], device_id=(dd, y), device_id_type=MESH)
             for kk, dd in ((kh0, down0), (kh1, down1))]

    @pl.when(gives)
    def _():
        halos[0].start()
        halos[1].start()

    heads[0].start()
    heads[1].start()
    for c in wcopies[4:]:
        c.wait()
    oth0 = pl.multiple_of(R - R * h, R)
    outs = []

    def go(src, dst, k, dt, dy=y):
        c = send(src, dst, k, dt, dy)
        c.start()
        outs.append(c)

    kry = [sem() for _ in range(3)]
    ycopies = {d: send(acc.at[pl.ds(pl.multiple_of(yn[d] * 256, 256), 256)], ry.at[d - 1], kry[d - 1], tm, yn[d])
               for d in (2, 1, 3)}
    HR = R // 2
    for half in range(2):
        if half == 1:
            @pl.when(jnp.logical_not(takes))
            def _():
                halo[...] = jnp.zeros((64, CH), F32)

            @pl.when(takes)
            def _():
                arrived(halo, kh0)

            arrived(xe.at[pl.ds(oth0, 64)], ks0)
            prep_x(12)

        @pl.loop(0, 8)
        def _(p):
            slot = p % 2
            res = jnp.dot(xcat[pl.ds(HR * half, HR + 16)], rhs[slot], preferred_element_type=F32)
            yb[0] = res[:, :K]
            yb[1] = res[:, K:]
            prep_w((p + 1) % 8, 1 - slot)
            acc[pl.ds(HR * half, HR)] += yb[0, pl.ds(2 * p, HR), :] + yb[1, pl.ds(2 * p + 1, HR), :]

        for d in (2, 1, 3):
            pl.when(yn[d] // 2 == half)(ycopies[d].start)
    outs.extend(ycopies.values())
    arrived(xe.at[pl.ds(pl.multiple_of(oth0 + 64, 64), R - 64)], ks1)

    order = (2, 1, 3, 0)
    shift = [16 * ((x + o) % 4) for o in order]

    def xprep(i):
        cols = pl.multiple_of(128 * i, 128)
        for a in range(A):
            v = xe[pl.ds(pl.multiple_of(128 * i + shift[a], 16), 128), :].T
            hi, lo = halves(v)
            rows = pl.ds(a * CH, CH)
            xt[rows, pl.ds(cols, 128)] = hi
            xt[rows, pl.ds(pl.multiple_of(PR + cols, 128), 128)] = hi
            xt[rows, pl.ds(pl.multiple_of(2 * PR + cols, 128), 128)] = lo

    for a in range(A):
        v = xe[pl.ds(pl.multiple_of(PR + shift[a], 16), 16), :]
        hi = v.astype(BF16).astype(F32)
        t = jnp.concatenate([hi, hi, v - hi, jnp.zeros((80, CH), F32)], axis=0)
        xt[pl.ds(a * CH, CH), pl.ds(3 * PR, 128)] = t.T.astype(BF16)
    pl.loop(0, 8)(xprep)
    for d in range(1, 4):
        arrived(ry.at[d - 1], kry[d - 1])
    own_q = pl.ds(pl.multiple_of(y * 256, 256), 256)
    mine = pl.ds(pl.multiple_of(16 + R * h + 256 * y, 16), 256)
    s_ext[mine] = (acc[own_q] + ry[0]) + (ry[1] + ry[2])

    kag = [sem() for _ in range(3)]
    kfw = [sem() for _ in range(4)]
    kge = [sem() for _ in range(7)]
    kgx = [sem() for _ in range(3)]
    kgz = [sem() for _ in range(3)]
    kgb = [sem() for _ in range(7)]

    def place(hh, yy):
        return s_ext.at[pl.ds(pl.multiple_of(16 + R * hh + 256 * yy, 16), 256)]

    def piece(hh, yy):
        return pl.ds(pl.multiple_of((hh * NY + yy) * 16, 16), 16)

    for d in (2, 1, 3):
        go(place(h, y), place(h, y), kag[d - 1], tm, yn[d])
    go(place(h, y), place(h, y), kfw[0], sib)
    sv = s_ext[mine]
    gm[...] = lax.dot_general(sv, sv, TN_DOT, precision=HI, preferred_element_type=F32)
    eight = [(0, 1), (0, 2), (0, 3), (1, 0), (1, 1), (1, 2), (1, 3)]
    hs, ts = (h, 1 - h), (tm, sib)
    for i, (o, d) in enumerate(eight):
        go(gm.at[piece(hs[o], yn[d])], ge.at[i], kge[i], ts[o], yn[d])
    pl.loop(8, 16)(xprep)
    for i in range(7):
        arrived(ge.at[i], kge[i])
    gm[piece(h, y)] = (((gm[piece(h, y)] + ge[0]) + (ge[1] + ge[2])) + ((ge[3] + ge[4]) + (ge[5] + ge[6])))
    for d in range(1, 4):
        go(gm.at[piece(h, y)], gx.at[d - 1], kgx[d - 1], xn[d])
    for d in (1, 3, 2):
        src = place(h, (y + 4 - d) % NY)
        arrived(src, kag[d - 1])
        go(src, src, kfw[d], sib)
    for d in range(1, 4):
        arrived(gx.at[d - 1], kgx[d - 1])
    gz[3] = (gm[piece(h, y)] + gx[0]) + (gx[1] + gx[2])
    for d in range(1, 4):
        go(gz.at[3], gz.at[d - 1], kgz[d - 1], zn[d])
    for d in range(4):
        arrived(place(1 - h, (y + 4 - d) % NY), kfw[d])

    def prep_s(n, j, pair):
        for c in range(2):
            cs = pl.ds(128 * c, 128)
            off = 16 - j - 2 * h - 4 * ((z + order[2 * pair + c]) % NZ)
            hi, lo = halves(s_ext[pl.ds(off, PR), :])
            srhs[n, pl.ds(0, PR), cs] = hi
            srhs[n, pl.ds(PR, PR), cs] = lo
            srhs[n, pl.ds(2 * PR, PR), cs] = hi
            hi, lo = halves(s_ext[pl.ds(PR + off, 16), :])
            srhs[n, pl.ds(3 * PR, 16), cs] = hi
            srhs[n, pl.ds(3 * PR + 16, 16), cs] = lo
            srhs[n, pl.ds(3 * PR + 32, 16), cs] = hi
            srhs[n, pl.ds(3 * PR + 48, 80), cs] = jnp.zeros((80, K), BF16)

    def unit_p(t, u):
        rows = pl.ds(512 * u, 512)
        res = jnp.dot(xt[rows, :], srhs[t], preferred_element_type=F32)
        for c in range(2):
            cp[2 * t + c, rows, :] = res[:, 128 * c : 128 * c + 128]

    def unit_q(t, u):
        res = jnp.dot(xt[pl.ds(512 * t, 512), :], srhs[2 + u], preferred_element_type=F32)
        for m in range(2):
            for c in range(2):
                cp[4 + 2 * t + m, pl.ds(256 * (2 * u + c), 256), :] = res[256 * m : 256 * m + 256, 128 * c : 128 * c + 128]

    rk = [[sem() for _ in range(6)] for _ in range(8)]

    def ends(n):
        return (xn[1], xn[3]) if n < 4 else (zn[1], zn[3])

    def first(n, u):
        up, dn = ends(n)
        src, buf = cp.at[n], xr.at[n]
        if u == 0:
            go(src.at[0:128], buf.at[0], rk[n][0], up)
            go(src.at[128:256], buf.at[1], rk[n][1], dn)
            go(src.at[384:512], buf.at[3], rk[n][3], up)
        else:
            go(src.at[512:640], buf.at[2], rk[n][2], dn)

    def second(n):
        up, dn = ends(n)
        arrived(xr.at[n, 0], rk[n][0])
        cp[n, 256:384] += xr[n, 0]
        go(cp.at[n, 256:384], xr.at[n, 4], rk[n][4], up)
        arrived(xr.at[n, 1], rk[n][1])
        cp[n, 640:768] += xr[n, 1]
        go(cp.at[n, 640:768], xr.at[n, 5], rk[n][5], dn)

    def last(n, dst):
        for i in (2, 3, 4, 5):
            arrived(xr.at[n, i], rk[n][i])
        dst[0:128] = cp[n, 768:896] + (xr[n, 2] + xr[n, 4])
        dst[128:256] = cp[n, 896:1024] + (xr[n, 3] + xr[n, 5])

    zk = [[sem() for _ in range(6)] for _ in range(2)]

    def part(q, t, src, dst=None):
        up, dn = ends(0 if q else 4)
        buf, ks = (pz, qz)[q], zk[q]
        a, b = pl.ds(0, 128), pl.ds(128, 128)
        if t == 0:
            go(src.at[a], buf.at[0], ks[0], up)
            go(src.at[b], buf.at[1], ks[1], dn)
        elif t == 1:
            go(src.at[b], buf.at[3], ks[3], up)
            arrived(buf.at[0], ks[0])
            src[a] += buf[0]
            go(src.at[a], buf.at[4], ks[4], up)
        elif t == 2:
            go(src.at[a], buf.at[2], ks[2], dn)
            arrived(buf.at[1], ks[1])
            src[b] += buf[1]
            go(src.at[b], buf.at[5], ks[5], dn)
        else:
            for i in (2, 3, 4, 5):
                arrived(buf.at[i], ks[i])
            dst[a] = src[a] + (buf[2] + buf[4])
            dst[b] = src[b] + (buf[3] + buf[5])

    prep_s(0, 0, 0)
    unit_p(0, 0)
    first(0, 0)
    first(1, 0)
    for d in range(1, 4):
        arrived(gz.at[d - 1], kgz[d - 1])
    gb[piece(h, y)] = (gz[3] + gz[0]) + (gz[1] + gz[2])
    for i, (o, d) in enumerate(eight):
        go(gb.at[piece(h, y)], gb.at[piece(h, y)], kgb[i], ts[o], yn[d])
    prep_s(2, 1, 0)
    unit_q(0, 0)
    first(4, 0)
    first(5, 0)
    prep_s(3, 1, 1)
    unit_p(0, 1)
    first(0, 1)
    first(1, 1)
    for i, (o, d) in enumerate(eight):
        arrived(gb.at[piece(hs[o], (y + 4 - d) % NY)], kgb[i])
    gw[...] = gb[...]
    eye(li)
    prep_s(1, 0, 1)
    factor(gw, li, FAC[0])
    unit_q(0, 1)
    first(4, 1)
    first(5, 1)
    second(0)
    second(1)
    factor(gw, li, FAC[1])
    unit_p(1, 0)
    first(2, 0)
    first(3, 0)
    second(4)
    second(5)
    factor(gw, li, FAC[2])
    unit_q(1, 0)
    first(6, 0)
    first(7, 0)
    factor(gw, li, FAC[3])
    unit_p(1, 1)
    first(2, 1)
    first(3, 1)
    last(0, p1.at[0])
    part(0, 0, p1.at[0])
    last(1, p1.at[1])
    part(0, 1, p1.at[1])
    factor(gw, li, FAC[4])
    unit_q(1, 1)
    first(6, 1)
    first(7, 1)
    second(2)
    second(3)
    last(4, q1.at[0])
    part(1, 0, q1.at[0])
    last(5, q1.at[1])
    part(1, 1, q1.at[1])
    second(6)
    second(7)
    factor(gw, li, FAC[5])
    root = float(NX * NZ * PR) ** 0.5
    own_s = s_ext[pl.ds(pl.multiple_of(16 + R * h, 16), R), :]
    basis_o[...] = lax.dot_general(own_s, li[...], NT_DOT, precision=HI, preferred_element_type=F32) * root
    last(2, p1.at[2])
    part(0, 2, p1.at[2])
    last(6, q1.at[2])
    part(1, 2, q1.at[2])
    last(3, p1.at[3])
    last(7, q1.at[3])
    part(0, 3, p1.at[3], raw.at[0])
    part(1, 3, q1.at[3], raw.at[1])
    for j in range(2):
        coef_o[j] = lax.dot_general(raw[j], li[...], NT_DOT, precision=HI, preferred_element_type=F32)

    for c in outs:
        c.wait_send()
    heads[0].wait_send()
    heads[1].wait_send()

    @pl.when(gives)
    def _():
        halos[0].wait_send()
        halos[1].wait_send()


FAC = (range(0, 3), range(3, 6), range(6, 9), range(9, 12), range(12, 16), range(16, 16))


def eye(li):
    rows = lax.broadcasted_iota(jnp.int32, (K, K), 0)
    cols = lax.broadcasted_iota(jnp.int32, (K, K), 1)
    li[...] = jnp.where(rows == cols, 1.0, 0.0).astype(F32)


def factor(g, li, blocks):
    for jb in blocks:
        base = 8 * jb
        rows = lax.broadcasted_iota(jnp.int32, (K - base, 1), 0)
        av, bv = g[base:], li[base:]
        for j in range(8):
            at_j = slice(base + j, base + j + 1)
            r = lax.rsqrt(av[j : j + 1, at_j])
            ra, rb = av[j : j + 1] * r, bv[j : j + 1] * r
            f = jnp.where(rows > j, av[:, at_j] * r, 0.0)
            av = av - f * ra
            bv = jnp.where(rows == j, rb, bv - f * rb)
        g[base:] = av
        li[base:] = bv


N_SEM = 4 + 3 + 3 + 4 + 48 + 12 + 7 + 3 + 3 + 7


def on_device(record, test_matrix):
    V = pl.BlockSpec(memory_space=pltpu.VMEM)
    H = pl.BlockSpec(memory_space=pl.ANY)
    return pl.pallas_call(
        body,
        out_shape=(jax.ShapeDtypeStruct((R, K), F32), jax.ShapeDtypeStruct((2, CH, K), F32)),
        in_specs=[H, H],
        out_specs=(V, V),
        scratch_shapes=[
            pltpu.VMEM((PR + 64, CH), F32),
            pltpu.VMEM((8, A, 2, CH, K), F32),
            pltpu.VMEM((R + 16, KC), BF16),
            pltpu.VMEM((2, KC, 2 * K), BF16),
            pltpu.VMEM((2, R // 2 + 16, K), F32),
            pltpu.VMEM((R, K), F32),
            pltpu.VMEM((3, 256, K), F32),
            pltpu.VMEM((PR + 32, K), F32),
            pltpu.VMEM((A * CH, KT), BF16),
            pltpu.VMEM((4, KT, 2 * K), BF16),
            pltpu.VMEM((8, A * CH, K), F32),
            pltpu.VMEM((8, 6, 128, K), F32),
            pltpu.VMEM((4, CH, K), F32),
            pltpu.VMEM((4, CH, K), F32),
            pltpu.VMEM((6, 128, K), F32),
            pltpu.VMEM((6, 128, K), F32),
            pltpu.VMEM((2, CH, K), F32),
            pltpu.VMEM((K, K), F32),
            pltpu.VMEM((7, 16, K), F32),
            pltpu.VMEM((3, 16, K), F32),
            pltpu.VMEM((4, 16, K), F32),
            pltpu.VMEM((K, K), F32),
            pltpu.VMEM((K, K), F32),
            pltpu.VMEM((K, K), F32),
            pltpu.SemaphoreType.DMA((33,)),
            pltpu.SemaphoreType.DMA((N_SEM,)),
            pltpu.SemaphoreType.DMA((N_SEM,)),
        ],
        compiler_params=pltpu.CompilerParams(collective_id=0, has_side_effects=True, vmem_limit_bytes=60 * 2**20),
    )(record, test_matrix)


def solution(mesh):
    return jax.shard_map(
        on_device,
        mesh=mesh,
        in_specs=(P("tm", "chan"), P(None, "chan", None)),
        out_specs=(P("tm", None), P("tm", "chan", None)),
        check_vma=False,
    )
```

time: 103 us -> 108 us (1.049)
  Pallas kernels: 98.9 us -> 104 us
    pallas_call x1, Pallas kernels: 98.9 us -> 104 us  [on_device(): pl.pallas_call(body, out_shape=(jax.ShapeDtypeStruct((R, K), F32), jax.Sh...]
where the time goes in v1:
time: 108 us
  Pallas kernels  104 us (96%)
  local copies, waits for them, and re-layouts  3.54 us (3%)
    pallas_call x1, Pallas kernels, on_device(): pl.pallas_call(body, out_shape=(jax.ShapeDtypeStruct((R, K), F32), jax.Sh...  104 us
    unnamed x2, local copies, waits for them, and re-layouts  3.54 us

profile of v1, /device:TPU:0, one launch (start us, length us, event | category | flops | bytes accessed | tf_op | source)
XLA Modules:
  0.0 107.8 jit_solution(18035448904672282865)
XLA Ops:
  0.6 103.6 %shard_map.41 = (f32[1024,128]{1,0:T(8,128)}, f32[2,256,128]{2,1,0:T(8,128)}) custom-call(f32[1024,256]{1,0:T(8,128)} %rec.1, f32[64,256,128]{2,1,0:T(8,128)} %w.1), custom_call_target="tpu_custom_call" | custom-call | tf_op jit(solution)/shard_map/pallas_call | solution.py:437
  104.2 1.9 %copy.6 = f32[1024,128]{1,0:T(8,128)} copy(f32[1024,128]{1,0:T(8,128)} %get-tuple-element.4) | data formatting | bytes 1048576
  106.1 1.7 %copy.7 = f32[2,256,128]{2,1,0:T(8,128)} copy(f32[2,256,128]{2,1,0:T(8,128)} %get-tuple-element.5) | data formatting | bytes 524288

commit v2 on v1

--- a/solution.py
+++ b/solution.py
@@ -211,25 +211,30 @@
     def piece(hh, yy):
         return pl.ds(pl.multiple_of((hh * NY + yy) * 16, 16), 16)
 
-    for d in (2, 1, 3):
-        go(place(h, y), place(h, y), kag[d - 1], tm, yn[d])
-    go(place(h, y), place(h, y), kfw[0], sib)
     sv = s_ext[mine]
     gm[...] = lax.dot_general(sv, sv, TN_DOT, precision=HI, preferred_element_type=F32)
     eight = [(0, 1), (0, 2), (0, 3), (1, 0), (1, 1), (1, 2), (1, 3)]
     hs, ts = (h, 1 - h), (tm, sib)
     for i, (o, d) in enumerate(eight):
         go(gm.at[piece(hs[o], yn[d])], ge.at[i], kge[i], ts[o], yn[d])
+    go(place(h, y), place(h, y), kfw[0], sib)
+    for d in (2, 1, 3):
+        go(place(h, y), place(h, y), kag[d - 1], tm, yn[d])
     pl.loop(8, 16)(xprep)
     for i in range(7):
         arrived(ge.at[i], kge[i])
     gm[piece(h, y)] = (((gm[piece(h, y)] + ge[0]) + (ge[1] + ge[2])) + ((ge[3] + ge[4]) + (ge[5] + ge[6])))
     for d in range(1, 4):
         go(gm.at[piece(h, y)], gx.at[d - 1], kgx[d - 1], xn[d])
-    for d in (1, 3, 2):
+
+    def forward(d):
         src = place(h, (y + 4 - d) % NY)
         arrived(src, kag[d - 1])
         go(src, src, kfw[d], sib)
+
+    forward(1)
+    forward(3)
+    forward(2)
     for d in range(1, 4):
         arrived(gx.at[d - 1], kgx[d - 1])
     gz[3] = (gm[piece(h, y)] + gx[0]) + (gx[1] + gx[2])
@@ -296,28 +301,40 @@
 
     zk = [[sem() for _ in range(6)] for _ in range(2)]
 
-    def part(q, t, src, dst=None):
+    def part_own(q, t, src):
         up, dn = ends(0 if q else 4)
         buf, ks = (pz, qz)[q], zk[q]
-        a, b = pl.ds(0, 128), pl.ds(128, 128)
+        a, b = src.at[0:128], src.at[128:256]
         if t == 0:
-            go(src.at[a], buf.at[0], ks[0], up)
-            go(src.at[b], buf.at[1], ks[1], dn)
+            go(a, buf.at[0], ks[0], up)
+            go(b, buf.at[1], ks[1], dn)
         elif t == 1:
-            go(src.at[b], buf.at[3], ks[3], up)
-            arrived(buf.at[0], ks[0])
-            src[a] += buf[0]
-            go(src.at[a], buf.at[4], ks[4], up)
-        elif t == 2:
-            go(src.at[a], buf.at[2], ks[2], dn)
-            arrived(buf.at[1], ks[1])
-            src[b] += buf[1]
-            go(src.at[b], buf.at[5], ks[5], dn)
+            go(b, buf.at[3], ks[3], up)
         else:
-            for i in (2, 3, 4, 5):
-                arrived(buf.at[i], ks[i])
-            dst[a] = src[a] + (buf[2] + buf[4])
-            dst[b] = src[b] + (buf[3] + buf[5])
+            go(a, buf.at[2], ks[2], dn)
+
+    def part_on(q, t, src):
+        up, dn = ends(0 if q else 4)
+        buf, ks = (pz, qz)[q], zk[q]
+        half, to = (pl.ds(0, 128), up) if t == 1 else (pl.ds(128, 128), dn)
+        arrived(buf.at[t - 1], ks[t - 1])
+        src[half] += buf[t - 1]
+        go(src.at[half], buf.at[3 + t], ks[3 + t], to)
+
+    def part_sum(q, src, dst):
+        buf, ks = (pz, qz)[q], zk[q]
+        for i in (2, 3, 4, 5):
+            arrived(buf.at[i], ks[i])
+        dst[0:128] = src[0:128] + (buf[2] + buf[4])
+        dst[128:256] = src[128:256] + (buf[3] + buf[5])
+
+    def p_last(n):
+        last(n, p1.at[n])
+        part_own(0, n, p1.at[n])
+
+    def q_last(n):
+        last(4 + n, q1.at[n])
+        part_own(1, n, q1.at[n])
 
     prep_s(0, 0, 0)
     unit_p(0, 0)
@@ -357,38 +374,35 @@
     unit_q(1, 0)
     first(6, 0)
     first(7, 0)
+    p_last(0)
+    p_last(1)
     factor(gw, li, FAC[3])
     unit_p(1, 1)
     first(2, 1)
     first(3, 1)
-    last(0, p1.at[0])
-    part(0, 0, p1.at[0])
-    last(1, p1.at[1])
-    part(0, 1, p1.at[1])
+    second(2)
+    second(3)
+    q_last(0)
+    q_last(1)
     factor(gw, li, FAC[4])
     unit_q(1, 1)
     first(6, 1)
     first(7, 1)
-    second(2)
-    second(3)
-    last(4, q1.at[0])
-    part(1, 0, q1.at[0])
-    last(5, q1.at[1])
-    part(1, 1, q1.at[1])
     second(6)
     second(7)
-    factor(gw, li, FAC[5])
+    part_on(0, 1, p1.at[1])
+    part_on(1, 1, q1.at[1])
     root = float(NX * NZ * PR) ** 0.5
     own_s = s_ext[pl.ds(pl.multiple_of(16 + R * h, 16), R), :]
     basis_o[...] = lax.dot_general(own_s, li[...], NT_DOT, precision=HI, preferred_element_type=F32) * root
-    last(2, p1.at[2])
-    part(0, 2, p1.at[2])
-    last(6, q1.at[2])
-    part(1, 2, q1.at[2])
+    p_last(2)
+    part_on(0, 2, p1.at[2])
+    q_last(2)
+    part_on(1, 2, q1.at[2])
     last(3, p1.at[3])
     last(7, q1.at[3])
-    part(0, 3, p1.at[3], raw.at[0])
-    part(1, 3, q1.at[3], raw.at[1])
+    part_sum(0, p1.at[3], raw.at[0])
+    part_sum(1, q1.at[3], raw.at[1])
     for j in range(2):
         coef_o[j] = lax.dot_general(raw[j], li[...], NT_DOT, precision=HI, preferred_element_type=F32)
 
@@ -403,7 +417,7 @@
         halos[1].wait_send()
 
 
-FAC = (range(0, 3), range(3, 6), range(6, 9), range(9, 12), range(12, 16), range(16, 16))
+FAC = (range(0, 3), range(3, 6), range(6, 9), range(9, 12), range(12, 16))
 
 
 def eye(li):

time: 108 us -> 96.8 us (0.90)
  Pallas kernels: 104 us -> 92.5 us
    pallas_call x1, Pallas kernels: 104 us -> 92.5 us  [on_device(): pl.pallas_call(body, out_shape=(jax.ShapeDtypeStruct((R, K), F32), jax.Sh...]
where the time goes in v2:
time: 96.8 us; the launch traced here: 96.6 us
  Pallas kernels  92.5 us (96%)
  local copies, waits for them, and re-layouts  3.54 us (4%)
    pallas_call x1, Pallas kernels, on_device(): pl.pallas_call(body, out_shape=(jax.ShapeDtypeStruct((R, K), F32), jax.Sh...  92.5 us
    unnamed x2, local copies, waits for them, and re-layouts  3.54 us

profile of v2, /device:TPU:0, one launch (start us, length us, event | category | flops | bytes accessed | tf_op | source)
XLA Modules:
  0.0 96.6 jit_solution(1538669262916479829)
XLA Ops:
  0.6 92.5 %shard_map.41 = (f32[1024,128]{1,0:T(8,128)}, f32[2,256,128]{2,1,0:T(8,128)}) custom-call(f32[1024,256]{1,0:T(8,128)} %rec.1, f32[64,256,128]{2,1,0:T(8,128)} %w.1), custom_call_target="tpu_custom_call" | custom-call | tf_op jit(solution)/shard_map/pallas_call | solution.py:451
  93.1 1.9 %copy.6 = f32[1024,128]{1,0:T(8,128)} copy(f32[1024,128]{1,0:T(8,128)} %get-tuple-element.4) | data formatting | bytes 1048576
  95.0 1.7 %copy.7 = f32[2,256,128]{2,1,0:T(8,128)} copy(f32[2,256,128]{2,1,0:T(8,128)} %get-tuple-element.5) | data formatting | bytes 524288

commit v3 on v2

--- a/solution.py
+++ b/solution.py
@@ -24,8 +24,8 @@
     return hi, (v - hi.astype(F32)).astype(BF16)
 
 
-def body(rec, w, basis_o, coef_o, xe, wf, xcat, rhs, yb, acc, ry, s_ext, xt, srhs, cp,
-         xr, p1, q1, pz, qz, raw, gm, ge, gx, gz, gb, gw, li, lsem, ss, rs):
+def body(rec, w, s_o, raw, li_o, xe, wf, xcat, rhs, yb, acc, ry, s_ext, xt, srhs, cp,
+         xr, p1, q1, pz, qz, gm, ge, gx, gz, gb, gw, li, lsem, ss, rs):
     tm = lax.axis_index("tm")
     y = lax.axis_index("chan")
     h = tm % 2
@@ -221,25 +221,19 @@
     for d in (2, 1, 3):
         go(place(h, y), place(h, y), kag[d - 1], tm, yn[d])
     pl.loop(8, 16)(xprep)
+    def forward(d):
+        src = place(h, (y + 4 - d) % NY)
+        arrived(src, kag[d - 1])
+        go(src, src, kfw[d], sib)
+
+    forward(1)
+    forward(3)
+    forward(2)
     for i in range(7):
         arrived(ge.at[i], kge[i])
     gm[piece(h, y)] = (((gm[piece(h, y)] + ge[0]) + (ge[1] + ge[2])) + ((ge[3] + ge[4]) + (ge[5] + ge[6])))
     for d in range(1, 4):
         go(gm.at[piece(h, y)], gx.at[d - 1], kgx[d - 1], xn[d])
-
-    def forward(d):
-        src = place(h, (y + 4 - d) % NY)
-        arrived(src, kag[d - 1])
-        go(src, src, kfw[d], sib)
-
-    forward(1)
-    forward(3)
-    forward(2)
-    for d in range(1, 4):
-        arrived(gx.at[d - 1], kgx[d - 1])
-    gz[3] = (gm[piece(h, y)] + gx[0]) + (gx[1] + gx[2])
-    for d in range(1, 4):
-        go(gz.at[3], gz.at[d - 1], kgz[d - 1], zn[d])
     for d in range(4):
         arrived(place(1 - h, (y + 4 - d) % NY), kfw[d])
 
@@ -341,14 +335,19 @@
     first(0, 0)
     first(1, 0)
     for d in range(1, 4):
+        arrived(gx.at[d - 1], kgx[d - 1])
+    gz[3] = (gm[piece(h, y)] + gx[0]) + (gx[1] + gx[2])
+    for d in range(1, 4):
+        go(gz.at[3], gz.at[d - 1], kgz[d - 1], zn[d])
+    prep_s(2, 1, 0)
+    unit_q(0, 0)
+    first(4, 0)
+    first(5, 0)
+    for d in range(1, 4):
         arrived(gz.at[d - 1], kgz[d - 1])
     gb[piece(h, y)] = (gz[3] + gz[0]) + (gz[1] + gz[2])
     for i, (o, d) in enumerate(eight):
         go(gb.at[piece(h, y)], gb.at[piece(h, y)], kgb[i], ts[o], yn[d])
-    prep_s(2, 1, 0)
-    unit_q(0, 0)
-    first(4, 0)
-    first(5, 0)
     prep_s(3, 1, 1)
     unit_p(0, 1)
     first(0, 1)
@@ -392,9 +391,8 @@
     second(7)
     part_on(0, 1, p1.at[1])
     part_on(1, 1, q1.at[1])
-    root = float(NX * NZ * PR) ** 0.5
-    own_s = s_ext[pl.ds(pl.multiple_of(16 + R * h, 16), R), :]
-    basis_o[...] = lax.dot_general(own_s, li[...], NT_DOT, precision=HI, preferred_element_type=F32) * root
+    s_o[...] = s_ext[pl.ds(pl.multiple_of(16 + R * h, 16), R), :]
+    li_o[...] = li[...]
     p_last(2)
     part_on(0, 2, p1.at[2])
     q_last(2)
@@ -403,8 +401,6 @@
     last(7, q1.at[3])
     part_sum(0, p1.at[3], raw.at[0])
     part_sum(1, q1.at[3], raw.at[1])
-    for j in range(2):
-        coef_o[j] = lax.dot_general(raw[j], li[...], NT_DOT, precision=HI, preferred_element_type=F32)
 
     for c in outs:
         c.wait_send()
@@ -418,6 +414,13 @@
 
 
 FAC = (range(0, 3), range(3, 6), range(6, 9), range(9, 12), range(12, 16))
+
+
+def apply_inverse(own, raw, inv, basis, coeffs):
+    root = float(NX * NZ * PR) ** 0.5
+    basis[...] = lax.dot_general(own[...], inv[...], NT_DOT, precision=HI, preferred_element_type=F32) * root
+    for j in range(2):
+        coeffs[j] = lax.dot_general(raw[j], inv[...], NT_DOT, precision=HI, preferred_element_type=F32)
 
 
 def eye(li):
@@ -448,11 +451,15 @@
 def on_device(record, test_matrix):
     V = pl.BlockSpec(memory_space=pltpu.VMEM)
     H = pl.BlockSpec(memory_space=pl.ANY)
-    return pl.pallas_call(
+    own, raw, inv = pl.pallas_call(
         body,
-        out_shape=(jax.ShapeDtypeStruct((R, K), F32), jax.ShapeDtypeStruct((2, CH, K), F32)),
+        out_shape=(
+            jax.ShapeDtypeStruct((R, K), F32),
+            jax.ShapeDtypeStruct((2, CH, K), F32),
+            jax.ShapeDtypeStruct((K, K), F32),
+        ),
         in_specs=[H, H],
-        out_specs=(V, V),
+        out_specs=(V, V, V),
         scratch_shapes=[
             pltpu.VMEM((PR + 64, CH), F32),
             pltpu.VMEM((8, A, 2, CH, K), F32),
@@ -470,7 +477,6 @@
             pltpu.VMEM((4, CH, K), F32),
             pltpu.VMEM((6, 128, K), F32),
             pltpu.VMEM((6, 128, K), F32),
-            pltpu.VMEM((2, CH, K), F32),
             pltpu.VMEM((K, K), F32),
             pltpu.VMEM((7, 16, K), F32),
             pltpu.VMEM((3, 16, K), F32),
@@ -484,6 +490,12 @@
         ],
         compiler_params=pltpu.CompilerParams(collective_id=0, has_side_effects=True, vmem_limit_bytes=60 * 2**20),
     )(record, test_matrix)
+    return pl.pallas_call(
+        apply_inverse,
+        out_shape=(jax.ShapeDtypeStruct((R, K), F32), jax.ShapeDtypeStruct((2, CH, K), F32)),
+        in_specs=[V, V, V],
+        out_specs=(V, V),
+    )(own, raw, inv)
 
 
 def solution(mesh):

time: 96.8 us -> 95.6 us (0.988); the launches traced: 96.6 us -> 94.4 us
  local copies, waits for them, and re-layouts: 3.54 us -> 0 us
  Pallas kernels: 92.5 us -> 93.8 us
    unnamed x2 -> x0, local copies, waits for them, and re-layouts: 3.54 us -> none
    pallas_call x0 -> x1, Pallas kernels: none -> 2.8 us  [on_device(): pl.pallas_call(apply_inverse, out_shape=(jax.ShapeDtypeStruct((R, K), F32...]
    pallas_call x1, Pallas kernels: 92.5 us -> 91 us  [on_device(): pl.pallas_call(body, out_shape=(jax.ShapeDtypeStruct((R, K), F32), jax.Sh...]
where the time goes in v3:
time: 95.6 us; the launch traced here: 94.4 us
  Pallas kernels  93.8 us (98%)
    pallas_call x1, Pallas kernels, on_device(): pl.pallas_call(body, out_shape=(jax.ShapeDtypeStruct((R, K), F32), jax.Sh...  91 us
    pallas_call x1, Pallas kernels, on_device(): pl.pallas_call(apply_inverse, out_shape=(jax.ShapeDtypeStruct((R, K), F32...  2.8 us

profile of v3, /device:TPU:0, one launch (start us, length us, event | category | flops | bytes accessed | tf_op | source)
XLA Modules:
  0.0 94.4 jit_solution(17997867256929444057)
XLA Ops:
  0.6 91.0 %shard_map.41 = (f32[1024,128]{1,0:T(8,128)}, f32[2,256,128]{2,1,0:T(8,128)}, f32[128,128]{1,0:T(8,128)}) custom-call(f32[1024,256]{1,0:T(8,128)} %rec.1, f32[64,256,128]{2,1,0:T(8,128)} %w.1), custom_call_target="tpu_custom_call" | custom-call | tf_op jit(solution)/shard_map/pallas_call | solution.py:454
  91.6 2.8 %shard_map.42 = (f32[1024,128]{1,0:T(8,128)}, f32[2,256,128]{2,1,0:T(8,128)}) custom-call(f32[1024,128]{1,0:T(8,128)} %get-tuple-element.5.own, f32[2,256,128]{2,1,0:T(8,128)} %get-tuple-element.6.raw, f32[128,128]{1,0:T(8,128)} %get-tuple-element.7.inv), custom_call_target="tpu_custom_call" | custom-call | tf_op jit(solution)/shard_map/pallas_call | solution.py:493

commit v4 on v3

--- a/solution.py
+++ b/solution.py
@@ -237,10 +237,10 @@
     for d in range(4):
         arrived(place(1 - h, (y + 4 - d) % NY), kfw[d])
 
-    def prep_s(n, j, pair):
-        for c in range(2):
-            cs = pl.ds(128 * c, 128)
-            off = 16 - j - 2 * h - 4 * ((z + order[2 * pair + c]) % NZ)
+    def prep_s(n):
+        for j in range(2):
+            cs = pl.ds(128 * j, 128)
+            off = 16 - j - 2 * h - 4 * ((z + order[n]) % NZ)
             hi, lo = halves(s_ext[pl.ds(off, PR), :])
             srhs[n, pl.ds(0, PR), cs] = hi
             srhs[n, pl.ds(PR, PR), cs] = lo
@@ -251,41 +251,41 @@
             srhs[n, pl.ds(3 * PR + 32, 16), cs] = hi
             srhs[n, pl.ds(3 * PR + 48, 80), cs] = jnp.zeros((80, K), BF16)
 
-    def unit_p(t, u):
+    def unit(u, c):
         rows = pl.ds(512 * u, 512)
-        res = jnp.dot(xt[rows, :], srhs[t], preferred_element_type=F32)
-        for c in range(2):
-            cp[2 * t + c, rows, :] = res[:, 128 * c : 128 * c + 128]
-
-    def unit_q(t, u):
-        res = jnp.dot(xt[pl.ds(512 * t, 512), :], srhs[2 + u], preferred_element_type=F32)
+        res = jnp.dot(xt[rows, :], srhs[c], preferred_element_type=F32)
+        cp[c, rows, :] = res[:, :K]
         for m in range(2):
-            for c in range(2):
-                cp[4 + 2 * t + m, pl.ds(256 * (2 * u + c), 256), :] = res[256 * m : 256 * m + 256, 128 * c : 128 * c + 128]
+            cp[4 + 2 * u + m, pl.ds(256 * c, 256), :] = res[256 * m : 256 * m + 256, K:]
 
     rk = [[sem() for _ in range(6)] for _ in range(8)]
 
     def ends(n):
         return (xn[1], xn[3]) if n < 4 else (zn[1], zn[3])
 
-    def first(n, u):
-        up, dn = ends(n)
-        src, buf = cp.at[n], xr.at[n]
-        if u == 0:
-            go(src.at[0:128], buf.at[0], rk[n][0], up)
-            go(src.at[128:256], buf.at[1], rk[n][1], dn)
-            go(src.at[384:512], buf.at[3], rk[n][3], up)
-        else:
-            go(src.at[512:640], buf.at[2], rk[n][2], dn)
-
-    def second(n):
-        up, dn = ends(n)
-        arrived(xr.at[n, 0], rk[n][0])
-        cp[n, 256:384] += xr[n, 0]
-        go(cp.at[n, 256:384], xr.at[n, 4], rk[n][4], up)
-        arrived(xr.at[n, 1], rk[n][1])
-        cp[n, 640:768] += xr[n, 1]
-        go(cp.at[n, 640:768], xr.at[n, 5], rk[n][5], dn)
+    def first(i, *ns):
+        for n in ns:
+            up, dn = ends(n)
+            src, buf = cp.at[n], xr.at[n]
+            if i == 0:
+                go(src.at[0:128], buf.at[0], rk[n][0], up)
+                go(src.at[128:256], buf.at[1], rk[n][1], dn)
+            elif i == 1:
+                go(src.at[384:512], buf.at[3], rk[n][3], up)
+            else:
+                go(src.at[512:640], buf.at[2], rk[n][2], dn)
+
+    def second_a(*ns):
+        for n in ns:
+            arrived(xr.at[n, 0], rk[n][0])
+            cp[n, 256:384] += xr[n, 0]
+            go(cp.at[n, 256:384], xr.at[n, 4], rk[n][4], ends(n)[0])
+
+    def second_b(*ns):
+        for n in ns:
+            arrived(xr.at[n, 1], rk[n][1])
+            cp[n, 640:768] += xr[n, 1]
+            go(cp.at[n, 640:768], xr.at[n, 5], rk[n][5], ends(n)[1])
 
     def last(n, dst):
         for i in (2, 3, 4, 5):
@@ -330,8 +330,8 @@
         last(4 + n, q1.at[n])
         part_own(1, n, q1.at[n])
 
-    prep_s(0, 0, 0)
-    unit_p(0, 0)
+    prep_s(0)
+    unit(0, 0)
     first(0, 0)
     first(1, 0)
     for d in range(1, 4):
@@ -339,56 +339,58 @@
     gz[3] = (gm[piece(h, y)] + gx[0]) + (gx[1] + gx[2])
     for d in range(1, 4):
         go(gz.at[3], gz.at[d - 1], kgz[d - 1], zn[d])
-    prep_s(2, 1, 0)
-    unit_q(0, 0)
-    first(4, 0)
-    first(5, 0)
+    first(0, 4, 5)
+    prep_s(1)
+    unit(0, 1)
+    first(0, 1)
+    first(1, 1, 4, 5)
     for d in range(1, 4):
         arrived(gz.at[d - 1], kgz[d - 1])
     gb[piece(h, y)] = (gz[3] + gz[0]) + (gz[1] + gz[2])
     for i, (o, d) in enumerate(eight):
         go(gb.at[piece(h, y)], gb.at[piece(h, y)], kgb[i], ts[o], yn[d])
-    prep_s(3, 1, 1)
-    unit_p(0, 1)
-    first(0, 1)
-    first(1, 1)
+    prep_s(2)
+    unit(1, 0)
+    first(2, 0)
+    first(0, 6, 7)
+    second_a(0)
+    second_b(0)
     for i, (o, d) in enumerate(eight):
         arrived(gb.at[piece(hs[o], (y + 4 - d) % NY)], kgb[i])
     gw[...] = gb[...]
     eye(li)
-    prep_s(1, 0, 1)
+    prep_s(3)
     factor(gw, li, FAC[0])
-    unit_q(0, 1)
-    first(4, 1)
-    first(5, 1)
-    second(0)
-    second(1)
+    unit(1, 1)
+    first(2, 1)
+    first(1, 6, 7)
+    second_a(1, 4, 5)
+    second_b(1)
     factor(gw, li, FAC[1])
-    unit_p(1, 0)
-    first(2, 0)
-    first(3, 0)
-    second(4)
-    second(5)
+    unit(0, 2)
+    first(0, 2)
+    first(1, 2)
+    first(2, 4, 5)
+    second_b(4, 5)
+    second_a(6, 7)
     factor(gw, li, FAC[2])
-    unit_q(1, 0)
-    first(6, 0)
-    first(7, 0)
+    unit(0, 3)
+    first(0, 3)
+    first(1, 3)
     p_last(0)
     p_last(1)
     factor(gw, li, FAC[3])
-    unit_p(1, 1)
-    first(2, 1)
-    first(3, 1)
-    second(2)
-    second(3)
+    unit(1, 2)
+    first(2, 2, 6, 7)
+    second_a(2)
+    second_b(2, 6, 7)
     q_last(0)
     q_last(1)
     factor(gw, li, FAC[4])
-    unit_q(1, 1)
-    first(6, 1)
-    first(7, 1)
-    second(6)
-    second(7)
+    unit(1, 3)
+    first(2, 3)
+    second_a(3)
+    second_b(3)
     part_on(0, 1, p1.at[1])
     part_on(1, 1, q1.at[1])
     s_o[...] = s_ext[pl.ds(pl.multiple_of(16 + R * h, 16), R), :]

time: 95.6 us -> 92.9 us (0.972)
  Pallas kernels: 93.8 us -> 91.1 us
    pallas_call x1, Pallas kernels: 91 us -> 88.3 us  [on_device(): pl.pallas_call(body, out_shape=(jax.ShapeDtypeStruct((R, K), F32), jax.Sh...]
where the time goes in v4:
time: 92.9 us; the launch traced here: 91.7 us
  Pallas kernels  91.1 us (98%)
    pallas_call x1, Pallas kernels, on_device(): pl.pallas_call(body, out_shape=(jax.ShapeDtypeStruct((R, K), F32), jax.Sh...  88.3 us
    pallas_call x1, Pallas kernels, on_device(): pl.pallas_call(apply_inverse, out_shape=(jax.ShapeDtypeStruct((R, K), F32...  2.8 us

profile of v4, /device:TPU:0, one launch (start us, length us, event | category | flops | bytes accessed | tf_op | source)
XLA Modules:
  0.0 91.7 jit_solution(10238703805441520503)
XLA Ops:
  0.6 88.3 %shard_map.41 = (f32[1024,128]{1,0:T(8,128)}, f32[2,256,128]{2,1,0:T(8,128)}, f32[128,128]{1,0:T(8,128)}) custom-call(f32[1024,256]{1,0:T(8,128)} %rec.1, f32[64,256,128]{2,1,0:T(8,128)} %w.1), custom_call_target="tpu_custom_call" | custom-call | tf_op jit(solution)/shard_map/pallas_call | solution.py:456
  88.9 2.8 %shard_map.42 = (f32[1024,128]{1,0:T(8,128)}, f32[2,256,128]{2,1,0:T(8,128)}) custom-call(f32[1024,128]{1,0:T(8,128)} %get-tuple-element.5.own, f32[2,256,128]{2,1,0:T(8,128)} %get-tuple-element.6.raw, f32[128,128]{1,0:T(8,128)} %get-tuple-element.7.inv), custom_call_target="tpu_custom_call" | custom-call | tf_op jit(solution)/shard_map/pallas_call | solution.py:495

commit v5 on v4

--- a/solution.py
+++ b/solution.py
@@ -391,14 +391,14 @@
     first(2, 3)
     second_a(3)
     second_b(3)
+    p_last(2)
+    q_last(2)
     part_on(0, 1, p1.at[1])
     part_on(1, 1, q1.at[1])
+    part_on(0, 2, p1.at[2])
+    part_on(1, 2, q1.at[2])
     s_o[...] = s_ext[pl.ds(pl.multiple_of(16 + R * h, 16), R), :]
     li_o[...] = li[...]
-    p_last(2)
-    part_on(0, 2, p1.at[2])
-    q_last(2)
-    part_on(1, 2, q1.at[2])
     last(3, p1.at[3])
     last(7, q1.at[3])
     part_sum(0, p1.at[3], raw.at[0])

time: 92.9 us -> 92.9 us (level)
  no operation moved by 1% of the time
where the time goes in v5:
time: 92.9 us; the launch traced here: 91.7 us
  Pallas kernels  91.1 us (98%)
    pallas_call x1, Pallas kernels, on_device(): pl.pallas_call(body, out_shape=(jax.ShapeDtypeStruct((R, K), F32), jax.Sh...  88.3 us
    pallas_call x1, Pallas kernels, on_device(): pl.pallas_call(apply_inverse, out_shape=(jax.ShapeDtypeStruct((R, K), F32...  2.8 us

profile of v5, /device:TPU:0, one launch (start us, length us, event | category | flops | bytes accessed | tf_op | source)
XLA Modules:
  0.0 91.7 jit_solution(15602984302922714052)
XLA Ops:
  0.6 88.3 %shard_map.41 = (f32[1024,128]{1,0:T(8,128)}, f32[2,256,128]{2,1,0:T(8,128)}, f32[128,128]{1,0:T(8,128)}) custom-call(f32[1024,256]{1,0:T(8,128)} %rec.1, f32[64,256,128]{2,1,0:T(8,128)} %w.1), custom_call_target="tpu_custom_call" | custom-call | tf_op jit(solution)/shard_map/pallas_call | solution.py:456
  88.9 2.8 %shard_map.42 = (f32[1024,128]{1,0:T(8,128)}, f32[2,256,128]{2,1,0:T(8,128)}) custom-call(f32[1024,128]{1,0:T(8,128)} %get-tuple-element.5.own, f32[2,256,128]{2,1,0:T(8,128)} %get-tuple-element.6.raw, f32[128,128]{1,0:T(8,128)} %get-tuple-element.7.inv), custom_call_target="tpu_custom_call" | custom-call | tf_op jit(solution)/shard_map/pallas_call | solution.py:495

commit v6 on v4

--- a/solution.py
+++ b/solution.py
@@ -159,14 +159,15 @@
             arrived(xe.at[pl.ds(oth0, 64)], ks0)
             prep_x(12)
 
-        @pl.loop(0, 8)
-        def _(p):
-            slot = p % 2
-            res = jnp.dot(xcat[pl.ds(HR * half, HR + 16)], rhs[slot], preferred_element_type=F32)
-            yb[0] = res[:, :K]
-            yb[1] = res[:, K:]
-            prep_w((p + 1) % 8, 1 - slot)
-            acc[pl.ds(HR * half, HR)] += yb[0, pl.ds(2 * p, HR), :] + yb[1, pl.ds(2 * p + 1, HR), :]
+        @pl.loop(0, 4)
+        def _(pp):
+            for slot in range(2):
+                p = 2 * pp + slot
+                res = jnp.dot(xcat[pl.ds(HR * half, HR + 16)], rhs[slot], preferred_element_type=F32)
+                yb[2 * slot] = res[:, :K]
+                yb[2 * slot + 1] = res[:, K:]
+                prep_w((p + 1) % 8, 1 - slot)
+                acc[pl.ds(HR * half, HR)] += yb[2 * slot, pl.ds(2 * p, HR), :] + yb[2 * slot + 1, pl.ds(2 * p + 1, HR), :]
 
         for d in (2, 1, 3):
             pl.when(yn[d] // 2 == half)(ycopies[d].start)
@@ -467,7 +468,7 @@
             pltpu.VMEM((8, A, 2, CH, K), F32),
             pltpu.VMEM((R + 16, KC), BF16),
             pltpu.VMEM((2, KC, 2 * K), BF16),
-            pltpu.VMEM((2, R // 2 + 16, K), F32),
+            pltpu.VMEM((4, R // 2 + 16, K), F32),
             pltpu.VMEM((R, K), F32),
             pltpu.VMEM((3, 256, K), F32),
             pltpu.VMEM((PR + 32, K), F32),

time: 92.9 us -> 89.6 us (0.964)
  Pallas kernels: 91.1 us -> 87.8 us
    pallas_call x1, Pallas kernels: 88.3 us -> 85 us  [on_device(): pl.pallas_call(body, out_shape=(jax.ShapeDtypeStruct((R, K), F32), jax.Sh...]
where the time goes in v6:
time: 89.6 us; the launch traced here: 88.4 us
  Pallas kernels  87.8 us (98%)
    pallas_call x1, Pallas kernels, on_device(): pl.pallas_call(body, out_shape=(jax.ShapeDtypeStruct((R, K), F32), jax.Sh...  85 us
    pallas_call x1, Pallas kernels, on_device(): pl.pallas_call(apply_inverse, out_shape=(jax.ShapeDtypeStruct((R, K), F32...  2.8 us

profile of v6, /device:TPU:0, one launch (start us, length us, event | category | flops | bytes accessed | tf_op | source)
XLA Modules:
  0.0 88.4 jit_solution(533693302306837860)
XLA Ops:
  0.6 85.0 %shard_map.41 = (f32[1024,128]{1,0:T(8,128)}, f32[2,256,128]{2,1,0:T(8,128)}, f32[128,128]{1,0:T(8,128)}) custom-call(f32[1024,256]{1,0:T(8,128)} %rec.1, f32[64,256,128]{2,1,0:T(8,128)} %w.1), custom_call_target="tpu_custom_call" | custom-call | tf_op jit(solution)/shard_map/pallas_call | solution.py:457
  85.6 2.8 %shard_map.42 = (f32[1024,128]{1,0:T(8,128)}, f32[2,256,128]{2,1,0:T(8,128)}) custom-call(f32[1024,128]{1,0:T(8,128)} %get-tuple-element.5.own, f32[2,256,128]{2,1,0:T(8,128)} %get-tuple-element.6.raw, f32[128,128]{1,0:T(8,128)} %get-tuple-element.7.inv), custom_call_target="tpu_custom_call" | custom-call | tf_op jit(solution)/shard_map/pallas_call | solution.py:496
